TPU v7x, 32 devices: a whole 2x2x4 slice. The times are simulated.
32 devices in a mesh: seq: 16 (over z, y, core), head: 2 (over x).
Axes of the slice: x: 2, y: 2, z: 4, core: 2. Of those that a mesh axis runs over, the one named last changes fastest.
Arguments:
- query: bfloat16 [4096, 8, 4, 128], P('seq', None, 'head'), may hold values from -40 to 40
- key_in: bfloat16 [4096, 8, 128], P('seq', 'head'), may hold values from -16 to 16
- value: bfloat16 [4096, 8, 128], P('seq', 'head'), may hold values from -6 to 6
- grad_out: bfloat16 [4096, 8, 4, 128], P('seq', None, 'head'), may hold values from -6 to 6
- band_width: int32 [8, 4], P(None, 'head'), may hold values from 1 to 2, as said below
- stride_bits: int32 [4], replicated, may hold values from 0 to 3, each once
- partner_table: int32 [32, 4], P('seq'), may hold values from 0 to 1
Outputs:
- attn_out: bfloat16 [4096, 8, 4, 128], P('seq', None, 'head')
- grad_query: bfloat16 [4096, 8, 4, 128], P('seq', None, 'head')
- grad_key: bfloat16 [4096, 8, 128], P('seq', 'head')
- grad_value: bfloat16 [4096, 8, 128], P('seq', 'head')
Inputs may be any that keep to these rules, and one draw needn't show every extreme that they name: `band_width`: some query head has band width 1 and some has 2. `stride_bits`: each section flips a different bit.
All inputs are finite; a program needn't handle non-finite values.
Results may differ from a plain program's by a relative error of at most 0.023.
Values may be sent and summed in bfloat16 or wider, within the bound.
A program may use at most 192 MiB of HBM per device.

v0:
```python
import jax
import jax.numpy as jnp
from jax import lax
from jax.sharding import PartitionSpec as P

BLOCK = 128
BANDMAX = 2


def from_behind(value, axis, steps):
    count = lax.axis_size(axis)
    initial, last = (max(0, -steps), min(count, count - steps))
    return lax.ppermute(value, axis, [(source, source + steps) for source in range(initial, last)])


def extended_2(block, sides, width):
    for axis, dim in sides:
        count = lax.axis_size(axis)
        forward = [(i, i + 1) for i in range(count - 1)]
        backward = [(target, source) for source, target in forward]
        low = lax.ppermute(
            lax.slice_in_dim(block, block.shape[dim] - width, None, axis=dim), axis, forward
        )
        high = lax.ppermute(lax.slice_in_dim(block, 0, width, axis=dim), axis, backward)
        block = jnp.concatenate([low, block, high], axis=dim)
    return block


def swapped(value, axis, distance):
    return lax.ppermute(value, axis, [(i, i ^ 1 << distance) for i in range(lax.axis_size(axis))])


def attend(query_block, grad_block, key_block, value_block, valid_keys, score_scale):
    scores = (
        jnp.einsum("qhgd,khd->hgqk", query_block, key_block, preferred_element_type=jnp.float32)
        * score_scale
    )
    scores = jnp.where(valid_keys[:, :, None, :], scores, -jnp.inf)
    row_max = jnp.max(scores, axis=-1, keepdims=True)
    log_total = row_max + jnp.log(jnp.sum(jnp.exp(scores - row_max), axis=-1, keepdims=True))
    probability = jnp.exp(scores - log_total)
    weights = probability.astype(jnp.bfloat16)
    output = jnp.einsum(
        "hgqk,khd->qhgd", weights, value_block, preferred_element_type=jnp.float32
    ).astype(jnp.bfloat16)
    row_delta = jnp.sum(grad_block.astype(jnp.float32) * output.astype(jnp.float32), axis=-1)
    grad_prob = jnp.einsum(
        "qhgd,khd->hgqk", grad_block, value_block, preferred_element_type=jnp.float32
    )
    grad_score = (
        probability * (grad_prob - jnp.transpose(row_delta, (1, 2, 0))[..., None])
    ).astype(jnp.bfloat16)
    grad_q = (
        jnp.einsum("hgqk,khd->qhgd", grad_score, key_block, preferred_element_type=jnp.float32)
        * score_scale
    ).astype(jnp.bfloat16)
    grad_k = (
        jnp.einsum("hgqk,qhgd->khd", grad_score, query_block, preferred_element_type=jnp.float32)
        * score_scale
    )
    grad_v = jnp.einsum("hgqk,qhgd->khd", weights, grad_block, preferred_element_type=jnp.float32)
    return (output, grad_q, grad_k, grad_v)


def fold_rims(extended, rim_rows):
    rows_dev = extended.shape[1] - 2 * rim_rows
    inner = extended[:, rim_rows : rim_rows + rows_dev]
    from_right = from_behind(extended[:, :rim_rows].astype(jnp.bfloat16), "seq", -1).astype(
        jnp.float32
    )
    from_left = from_behind(
        extended[:, rim_rows + rows_dev :].astype(jnp.bfloat16), "seq", 1
    ).astype(jnp.float32)
    inner = inner.at[:, rows_dev - rim_rows :].add(from_right)
    inner = inner.at[:, :rim_rows].add(from_left)
    return inner


def shards(query, key_in, value, grad_out, band_width, stride_bits, partner_table):
    rows_dev = key_in.shape[0]
    head_dim = key_in.shape[2]
    groups_local = query.shape[2]
    local_blocks = rows_dev // BLOCK
    half_band = BANDMAX - 1
    rim_rows = half_band * BLOCK
    span_blocks = 2 * half_band + 1
    levels = lax.axis_size("seq").bit_length() - 1
    all_blocks = local_blocks * lax.axis_size("seq")
    score_scale = head_dim ** (-0.5)
    device = lax.axis_index("seq")
    stacked = jnp.stack([key_in, value])
    all_heads = lax.all_gather(stacked, "head", axis=2, tiled=True)
    extended = extended_2(all_heads, (("seq", 1),), rim_rows)
    received = [swapped(all_heads, "seq", level_bit) for level_bit in range(levels)]
    kv_heads = extended.shape[2]
    band_keys = jnp.stack(
        [
            extended[:, block_num * BLOCK : block_num * BLOCK + span_blocks * BLOCK]
            for block_num in range(local_blocks)
        ],
        axis=0,
    )
    chosen_list = []
    partner_list = []
    for level_bit in range(levels):
        section_match = (stride_bits == level_bit).astype(jnp.int32)
        chosen = jnp.sum(partner_table * section_match[None, :], axis=1)
        chosen_list.append(chosen)
        arriving = received[level_bit].reshape(2, local_blocks, BLOCK, kv_heads, head_dim)
        partner_list.append(jnp.take(arriving, chosen, axis=1))
    partner_keys = jnp.stack(partner_list, axis=2)
    partner_keys = jnp.swapaxes(partner_keys, 0, 1).reshape(
        local_blocks, 2, levels * BLOCK, kv_heads, head_dim
    )
    key_pairs = jnp.concatenate([band_keys, partner_keys], axis=2)
    offsets = jnp.arange(-half_band, half_band + 1, dtype=jnp.int32)
    global_blocks = device * local_blocks + jnp.arange(local_blocks, dtype=jnp.int32)
    nearby = global_blocks[:, None] + offsets[None, :]
    edge_valid = (nearby >= 0) & (nearby < all_blocks)
    width_valid = jnp.abs(offsets)[None, None, :] < band_width[:, :, None]
    band_valid = edge_valid[:, None, None, :] & width_valid[None]
    valid_all = jnp.concatenate(
        [band_valid, jnp.ones((local_blocks, kv_heads, groups_local, levels), jnp.bool_)], axis=-1
    )
    valid_all = jnp.repeat(valid_all, BLOCK, axis=-1)
    query_blocks = query.reshape(local_blocks, BLOCK, kv_heads, groups_local, head_dim)
    grad_blocks = grad_out.reshape(local_blocks, BLOCK, kv_heads, groups_local, head_dim)
    head_step = min(kv_heads, 4)

    def one_block(block_items):
        query_block, grad_block, key_pair, valid_keys = block_items
        results = [
            attend(
                query_block[:, head_start : head_start + head_step],
                grad_block[:, head_start : head_start + head_step],
                key_pair[0][:, head_start : head_start + head_step],
                key_pair[1][:, head_start : head_start + head_step],
                valid_keys[head_start : head_start + head_step],
                score_scale,
            )
            for head_start in range(0, kv_heads, head_step)
        ]
        return tuple(
            (jnp.concatenate([result[member] for result in results], axis=1) for member in range(4))
        )

    outputs, grad_queries, key_terms, value_terms = lax.map(
        one_block, (query_blocks, grad_blocks, key_pairs, valid_all)
    )
    band_total = jnp.zeros((2, rows_dev + 2 * rim_rows, kv_heads, head_dim), jnp.float32)
    for block_num in range(local_blocks):
        band_piece = jnp.stack(
            [
                key_terms[block_num, : span_blocks * BLOCK],
                value_terms[block_num, : span_blocks * BLOCK],
            ]
        )
        band_total = band_total.at[
            :, block_num * BLOCK : block_num * BLOCK + span_blocks * BLOCK
        ].add(band_piece)
    targets = jnp.arange(local_blocks, dtype=jnp.int32)
    partner_terms = []
    for level_bit in range(levels):
        first = (span_blocks + level_bit) * BLOCK
        level_part = jnp.stack(
            [key_terms[:, first : first + BLOCK], value_terms[:, first : first + BLOCK]], axis=1
        )
        routing = (chosen_list[level_bit][:, None] == targets[None, :]).astype(jnp.float32)
        routed = jnp.einsum("jt,jcbhd->ctbhd", routing, level_part, precision=lax.Precision.HIGHEST)
        partner_terms.append(routed.reshape(2, rows_dev, kv_heads, head_dim))
    total = fold_rims(band_total, rim_rows)
    for level_bit in range(levels):
        total = total + swapped(partner_terms[level_bit], "seq", level_bit)
    total = lax.psum_scatter(total, "head", scatter_dimension=2, tiled=True)
    return (
        outputs.reshape(query.shape),
        grad_queries.reshape(query.shape),
        total[0].astype(jnp.bfloat16),
        total[1].astype(jnp.bfloat16),
    )


def solution(mesh):
    placed = (
        P("seq", None, "head", None),
        P("seq", "head", None),
        P("seq", "head", None),
        P("seq", None, "head", None),
        P(None, "head"),
        P(),
        P("seq", None),
    )
    return jax.shard_map(
        shards,
        mesh=mesh,
        in_specs=placed,
        out_specs=(
            P("seq", None, "head", None),
            P("seq", None, "head", None),
            P("seq", "head", None),
            P("seq", "head", None),
        ),
        check_vma=False,
    )
```

profile of v0, /device:TPU:0, one launch (start us, length us, event | category | flops | bytes accessed | tf_op | source)
XLA Modules:
  0.0 421.4 jit_solution(7967060146923423590)
XLA Ops:
  11.7 22.4 %all-gather.2.cloned.1.call-done = bf16[2,256,8,128]{3,1,2,0:T(8,128)(2,1)} async-done(((bf16[2,256,4,128]{3,1,2,0:T(8,128)(2,1)}), bf16[2,256,8,128]{3,1,2,0:T(8,128)(2,1)}) %all-gather.2.cloned.1.call-update) | async-done | bytes 1048592 | tf_op jit(solution)/shard_map/all_gather | solution.py:92
  43.6 26.1 %collective-permute-start.4 = (bf16[2,256,8,128]{3,1,2,0:T(8,128)(2,1)}, bf16[2,256,8,128]{3,1,2,0:T(8,128)(2,1)}, u32[]{:S(2)}, u32[]{:S(2)}) collective-permute-start(bf16[2,256,8,128]{3,1,2,0:T(8,128)(2,1)} %all-gather.2.cloned.1.call-done), channel_id=1, source_target_pairs={{0,8},{2,10},{4,12},{6,14},{8,0},{10,2},{12,4},{14,6},{16,24},{18,... | collective-permute-start | bytes 3145736 | tf_op jit(solution)/shard_map/ppermute | solution.py:30
  77.8 7.2 %collective-permute-done.5 = bf16[2,256,8,128]{3,1,2,0:T(8,128)(2,1)} collective-permute-done((bf16[2,256,8,128]{3,1,2,0:T(8,128)(2,1)}, bf16[2,256,8,128]{3,1,2,0:T(8,128)(2,1)}, u32[]{:S(2)}, u32[]{:S(2)}) %collective-permute-start.5) | collective-permute-done | bytes 1048608 | tf_op jit(solution)/shard_map/ppermute | solution.py:30
  93.9 13.4 %collective-permute-done.4 = bf16[2,256,8,128]{3,1,2,0:T(8,128)(2,1)} collective-permute-done((bf16[2,256,8,128]{3,1,2,0:T(8,128)(2,1)}, bf16[2,256,8,128]{3,1,2,0:T(8,128)(2,1)}, u32[]{:S(2)}, u32[]{:S(2)}) %collective-permute-start.4) | collective-permute-done | bytes 1048608 | tf_op jit(solution)/shard_map/ppermute | solution.py:30
  113.9 3.8 pad_maximum_fusion
  117.6 81.9 %while.20 = (s32[]{:T(128)}, bf16[2,128,8,2,128]{4,3,2,1,0:T(2,128)(2,1)}, bf16[2,128,8,2,128]{4,3,2,1,0:T(2,128)(2,1)}, f32[2,896,8,128]{1,3,2,0:T(8,128)}, f32...) while((s32[]{:T(128)}, ...), condition=%wide.region_11.13_spmd, body=%wide.region_4.12_spmd.sunk | while | flops 2862215168 | bytes 108527856 | solution.py:147
  139.3 4.5 %convolution_bitcast_fusion.4 = f32[896,4,128]{0,2,1:T(8,128)} fusion(f32[4,896,128,2]{2,1,3,0:T(8,128)S(1)} %get-tuple-element.266, f32[4,2,128]{2,1,0:T(2,128)S(1)} %bitcast.380, pred[4,2,896]{2,1,0:T(4,128)(4,1)S(1)} %bitcast.365, bf16[1,128,8,2,128]{1,4,3,2,0:T(8,128)(2,1)S(1)} %copy.200), kind=kOutput, calls=%fused_computation.30.clone.1 | convolution fusion | flops 238551040 | bytes 6040576 | tf_op jit(solution)/shard_map/while/body/eval_jaxpr/hgqk,qhgd->khd/dot_general | solution.py:61
  152.9 5.6 %fusion.120 = (f32[2,896,8,128]{1,3,2,0:T(8,128)}, f32[2,896,8,128]{1,3,2,0:T(8,128)}) fusion(f32[2,896,8,128]{1,3,2,0:T(8,128)} %get-tuple-element.295, s32[]{:T(128)S(6)} %copy.213, f32[896,4,128]{0,2,1:T(8,128)} %fusion.118, f32[896,4,128]{0,2,1:T(8,128)} %fusion.119, f32[2,896,8,128]{1,3,2,0:T(8,128)} %get-tuple-element.296, ...), kind=kLoop, calls=%fused_computation.5.clone.1 | loop fusion | flops 1835008 | bytes 14680068 | tf_op jit(solution)/shard_map/while/body/jit(dynamic_update_index_in_dim)/dynamic_update_slice | solution.py:147
  180.2 4.5 %convolution_bitcast_fusion.4 = f32[896,4,128]{0,2,1:T(8,128)} fusion(f32[4,896,128,2]{2,1,3,0:T(8,128)S(1)} %get-tuple-element.266, f32[4,2,128]{2,1,0:T(2,128)S(1)} %bitcast.380, pred[4,2,896]{2,1,0:T(4,128)(4,1)S(1)} %bitcast.365, bf16[1,128,8,2,128]{1,4,3,2,0:T(8,128)(2,1)S(1)} %copy.200), kind=kOutput, calls=%fused_computation.30.clone.1 | convolution fusion | flops 238551040 | bytes 6040576 | tf_op jit(solution)/shard_map/while/body/eval_jaxpr/hgqk,qhgd->khd/dot_general | solution.py:61
  193.9 5.6 %fusion.120 = (f32[2,896,8,128]{1,3,2,0:T(8,128)}, f32[2,896,8,128]{1,3,2,0:T(8,128)}) fusion(f32[2,896,8,128]{1,3,2,0:T(8,128)} %get-tuple-element.295, s32[]{:T(128)S(6)} %copy.213, f32[896,4,128]{0,2,1:T(8,128)} %fusion.118, f32[896,4,128]{0,2,1:T(8,128)} %fusion.119, f32[2,896,8,128]{1,3,2,0:T(8,128)} %get-tuple-element.296, ...), kind=kLoop, calls=%fused_computation.5.clone.1 | loop fusion | flops 1835008 | bytes 14680068 | tf_op jit(solution)/shard_map/while/body/jit(dynamic_update_index_in_dim)/dynamic_update_slice | solution.py:147
  199.5 7.9 %copy.111 = f32[2,896,8,128]{3,2,1,0:T(8,128)} copy(f32[2,896,8,128]{1,3,2,0:T(8,128)} %get-tuple-element.106) | data formatting | bytes 14680064 | tf_op jit(solution)/shard_map/while | solution.py:147
  207.4 11.9 %copy.115 = f32[2,896,8,128]{3,0,2,1:T(2,128)} copy(f32[2,896,8,128]{1,3,2,0:T(8,128)} %get-tuple-element.106) | data formatting | bytes 14680064 | tf_op jit(solution)/shard_map/while | solution.py:147
  219.3 7.9 %copy.110 = f32[2,896,8,128]{3,2,1,0:T(8,128)} copy(f32[2,896,8,128]{1,3,2,0:T(8,128)} %get-tuple-element.105) | data formatting | bytes 14680064 | tf_op jit(solution)/shard_map/while | solution.py:147
  227.2 11.9 %copy.114 = f32[2,896,8,128]{3,0,2,1:T(2,128)} copy(f32[2,896,8,128]{1,3,2,0:T(8,128)} %get-tuple-element.105) | data formatting | bytes 14680064 | tf_op jit(solution)/shard_map/while | solution.py:147
  239.1 3.8 slice_bitcast_fusion.18
  244.9 5.7 %fusion.43 = f32[2,2,128,8,128]{4,1,3,2,0:T(2,128)S(1)} fusion(f32[2,1,128,8,128]{4,0,3,2,1:T(2,128)S(1)} %get-tuple-element.170, f32[2,1,128,8,128]{4,0,3,2,1:T(2,128)S(1)} %get-tuple-element.166, s32[2]{0:T(128)S(1)} %copy-done.11), kind=kOutput, calls=%fused_computation.93 | convolution fusion | flops 13107204 | bytes 4194312 | tf_op jit(solution)/shard_map/jt,jcbhd->ctbhd/dot_general | solution.py:169
  251.2 5.6 %fusion.46 = f32[2,2,128,8,128]{4,1,3,2,0:T(2,128)S(1)} fusion(f32[2,1,128,8,128]{4,0,3,2,1:T(2,128)S(1)} %get-tuple-element.171, f32[2,1,128,8,128]{4,0,3,2,1:T(2,128)S(1)} %get-tuple-element.167, s32[2]{0:T(128)S(1)} %copy-done.9), kind=kOutput, calls=%fused_computation.96 | convolution fusion | flops 13107204 | bytes 4194312 | tf_op jit(solution)/shard_map/jt,jcbhd->ctbhd/dot_general | solution.py:169
  257.5 5.6 %fusion.45 = f32[2,2,128,8,128]{4,1,3,2,0:T(2,128)S(1)} fusion(f32[2,1,128,8,128]{4,0,3,2,1:T(2,128)S(1)} %get-tuple-element.172, f32[2,1,128,8,128]{4,0,3,2,1:T(2,128)S(1)} %get-tuple-element.168, s32[2]{0:T(128)S(1)} %copy-done.7), kind=kOutput, calls=%fused_computation.95 | convolution fusion | flops 13107204 | bytes 4194312 | tf_op jit(solution)/shard_map/jt,jcbhd->ctbhd/dot_general | solution.py:169
  263.8 5.6 %fusion.44 = f32[2,2,128,8,128]{4,1,3,2,0:T(2,128)S(1)} fusion(f32[2,1,128,8,128]{4,0,3,2,1:T(2,128)S(1)} %get-tuple-element.173, f32[2,1,128,8,128]{4,0,3,2,1:T(2,128)S(1)} %get-tuple-element.169, s32[2]{0:T(128)S(1)} %copy-done.5), kind=kOutput, calls=%fused_computation.94 | convolution fusion | flops 13107204 | bytes 4194312 | tf_op jit(solution)/shard_map/jt,jcbhd->ctbhd/dot_general | solution.py:169
  269.8 4.7 %collective-permute-start.11 = (f32[2,256,8,128]{3,2,1,0:T(8,128)S(1)}, f32[2,256,8,128]{3,2,1,0:T(8,128)S(1)}, u32[]{:S(2)}, u32[]{:S(2)}) collective-permute-start(f32[2,256,8,128]{3,2,1,0:T(8,128)S(1)} %bitcast.358), channel_id=1, source_target_pairs={{0,16},{2,18},{4,20},{6,22},{8,24},{10,26},{12,28},{14,30},{16,0},... | collective-permute-start | bytes 6291464 | tf_op jit(solution)/shard_map/ppermute | solution.py:30
  282.6 42.4 %collective-permute-start.7 = (bf16[2,128,8,128]{3,2,1,0:T(8,128)(2,1)S(1)}, bf16[2,128,8,128]{3,2,1,0:T(8,128)(2,1)S(1)}, u32[]{:S(2)}, u32[]{:S(2)}) collective-permute-start(bf16[2,128,8,128]{3,2,1,0:T(8,128)(2,1)S(1)} %slice.334), channel_id=1, source_target_pairs={{0,2},{2,4},{4,6},{6,8},{8,10},{10,12},{12,14},{14,16},{16,18},{18... | collective-permute-start | bytes 1572872 | tf_op jit(solution)/shard_map/ppermute | solution.py:13
  326.7 27.8 %collective-permute-done.10 = f32[2,256,8,128]{3,2,1,0:T(8,128)S(1)} collective-permute-done((f32[2,256,8,128]{3,2,1,0:T(8,128)S(1)}, f32[2,256,8,128]{3,2,1,0:T(8,128)S(1)}, u32[]{:S(2)}, u32[]{:S(2)}) %collective-permute-start.10) | collective-permute-done | bytes 2097184 | tf_op jit(solution)/shard_map/ppermute | solution.py:30
  354.5 10.0 %collective-permute-done.11 = f32[2,256,8,128]{3,2,1,0:T(8,128)S(1)} collective-permute-done((f32[2,256,8,128]{3,2,1,0:T(8,128)S(1)}, f32[2,256,8,128]{3,2,1,0:T(8,128)S(1)}, u32[]{:S(2)}, u32[]{:S(2)}) %collective-permute-start.11) | collective-permute-done | bytes 2097184 | tf_op jit(solution)/shard_map/ppermute | solution.py:30
  366.8 44.7 %reduce-scatter.2.cloned.1.call-done = f32[2,256,4,128]{3,1,0,2:T(8,128)} async-done(((f32[2,256,8,128]{3,1,0,2:T(8,128)}), f32[2,256,4,128]{3,1,0,2:T(8,128)}) %reduce-scatter.2.cloned.1.call-update) | async-done | bytes 1048592 | tf_op jit(solution)/shard_map/reduce_scatter | solution.py:174
  (163 shorter events, 117.8 us)
Async XLA Ops:
  7.2 27.0 %all-gather.2.cloned.1.call-start = ((), (), s32[]{:S(2)}) async-start(), calls=%async_computation.1 | async-start | bytes 1572864 | tf_op jit(solution)/shard_map/all_gather | solution.py:92
  9.2 402.2 %reduce-scatter.2.cloned.1.call-start = ((), (), s32[]{:S(2)}) async-start(), calls=%async_computation.2 | async-start | bytes 3145728 | tf_op jit(solution)/shard_map/reduce_scatter | solution.py:174
  10.7 24.9 %copy-start.8 = (s32[2]{0:T(128)}, s32[2]{0:T(128)S(1)}, u32[]{:S(2)}) copy-start(s32[2]{0:T(128)S(1)} %get-tuple-element.133) | copy-start | bytes 28
  10.8 28.6 %copy-start.4 = (s32[2]{0:T(128)}, s32[2]{0:T(128)S(1)}, u32[]{:S(2)}) copy-start(s32[2]{0:T(128)S(1)} %get-tuple-element.132) | copy-start | bytes 28
  10.8 32.8 %copy-start.10 = (s32[2]{0:T(128)}, s32[2]{0:T(128)S(1)}, u32[]{:S(2)}) copy-start(s32[2]{0:T(128)S(1)} %get-tuple-element.131) | copy-start | bytes 28
  10.8 32.8 %copy-start.6 = (s32[2]{0:T(128)}, s32[2]{0:T(128)S(1)}, u32[]{:S(2)}) copy-start(s32[2]{0:T(128)S(1)} %get-tuple-element.134) | copy-start | bytes 28
  34.2 37.9 %collective-permute-start.3 = (bf16[2,256,8,128]{3,1,2,0:T(8,128)(2,1)}, bf16[2,256,8,128]{3,1,2,0:T(8,128)(2,1)}, u32[]{:S(2)}, u32[]{:S(2)}) collective-permute-start(bf16[2,256,8,128]{3,1,2,0:T(8,128)(2,1)} %all-gather.2.cloned.1.call-done), channel_id=1, source_target_pairs={{0,4},{2,6},{4,0},{6,2},{8,12},{10,14},{12,8},{14,10},{16,20},{18,... | collective-permute-start | bytes 3145736 | tf_op jit(solution)/shard_map/ppermute | solution.py:30
  35.6 39.3 %collective-permute-start.2 = (bf16[2,256,8,128]{3,1,2,0:T(8,128)(2,1)}, bf16[2,256,8,128]{3,1,2,0:T(8,128)(2,1)}, u32[]{:S(2)}, u32[]{:S(2)}) collective-permute-start(bf16[2,256,8,128]{3,1,2,0:T(8,128)(2,1)} %all-gather.2.cloned.1.call-done), channel_id=1, source_target_pairs={{0,2},{2,0},{4,6},{6,4},{8,10},{10,8},{12,14},{14,12},{16,18},{18,... | collective-permute-start | bytes 3145736 | tf_op jit(solution)/shard_map/ppermute | solution.py:30
  35.6 49.4 %collective-permute-start.5 = (bf16[2,256,8,128]{3,1,2,0:T(8,128)(2,1)}, bf16[2,256,8,128]{3,1,2,0:T(8,128)(2,1)}, u32[]{:S(2)}, u32[]{:S(2)}) collective-permute-start(bf16[2,256,8,128]{3,1,2,0:T(8,128)(2,1)} %all-gather.2.cloned.1.call-done), channel_id=1, source_target_pairs={{0,16},{2,18},{4,20},{6,22},{8,24},{10,26},{12,28},{14,30},{16,0},... | collective-permute-start | bytes 3145736 | tf_op jit(solution)/shard_map/ppermute | solution.py:30
  39.3 4.3 %collective-permute-start = (bf16[2,128,8,128]{3,1,2,0:T(8,128)(2,1)S(1)}, bf16[2,128,8,128]{3,1,2,0:T(8,128)(2,1)}, u32[]{:S(2)}, u32[]{:S(2)}) collective-permute-start(bf16[2,128,8,128]{3,1,2,0:T(8,128)(2,1)S(1)} %get-tuple-element.180), channel_id=1, source_target_pairs={{0,2},{2,4},{4,6},{6,8},{8,10},{10,12},{12,14},{14,16},{16,18},{18... | collective-permute-start | bytes 1572872 | tf_op jit(solution)/shard_map/ppermute | solution.py:21
  42.3 27.7 %collective-permute-start.1 = (bf16[2,128,8,128]{3,1,2,0:T(8,128)(2,1)S(1)}, bf16[2,128,8,128]{3,1,2,0:T(8,128)(2,1)}, u32[]{:S(2)}, u32[]{:S(2)}) collective-permute-start(bf16[2,128,8,128]{3,1,2,0:T(8,128)(2,1)S(1)} %get-tuple-element.181), channel_id=1, source_target_pairs={{2,0},{4,2},{6,4},{8,6},{10,8},{12,10},{14,12},{16,14},{18,16},{20... | collective-permute-start | bytes 1572872 | tf_op jit(solution)/shard_map/ppermute | solution.py:24
  43.6 63.7 %collective-permute-start.4 = (bf16[2,256,8,128]{3,1,2,0:T(8,128)(2,1)}, bf16[2,256,8,128]{3,1,2,0:T(8,128)(2,1)}, u32[]{:S(2)}, u32[]{:S(2)}) collective-permute-start(bf16[2,256,8,128]{3,1,2,0:T(8,128)(2,1)} %all-gather.2.cloned.1.call-done), channel_id=1, source_target_pairs={{0,8},{2,10},{4,12},{6,14},{8,0},{10,2},{12,4},{14,6},{16,24},{18,... | collective-permute-start | bytes 3145736 | tf_op jit(solution)/shard_map/ppermute | solution.py:30
  87.9 4.8 %copy-start.3 = (bf16[2,2,128,8,128]{4,2,3,1,0:T(8,128)(2,1)S(1)}, bf16[2,2,128,8,128]{4,2,3,1,0:T(8,128)(2,1)}, u32[]{:S(2)}) copy-start(bf16[2,2,128,8,128]{4,2,3,1,0:T(8,128)(2,1)} %gather_fusion.3) | copy-start | bytes 3145732
  132.9 3.1 copy-start.2
  151.2 1.7 copy-start
  173.8 3.1 copy-start.2
  192.1 1.7 copy-start
  239.1 4.3 %copy-start.1 = (f32[2,896,8,128]{3,0,2,1:T(2,128)S(1)}, f32[2,896,8,128]{3,0,2,1:T(2,128)}, u32[]{:S(2)}) copy-start(f32[2,896,8,128]{3,0,2,1:T(2,128)} %copy.114) | copy-start | bytes 22020100
  269.6 57.1 %collective-permute-start.9 = (f32[2,256,8,128]{3,2,1,0:T(8,128)S(1)}, f32[2,256,8,128]{3,2,1,0:T(8,128)S(1)}, u32[]{:S(2)}, u32[]{:S(2)}) collective-permute-start(f32[2,256,8,128]{3,2,1,0:T(8,128)S(1)} %bitcast.360), channel_id=1, source_target_pairs={{0,4},{2,6},{4,0},{6,2},{8,12},{10,14},{12,8},{14,10},{16,20},{18,... | collective-permute-start | bytes 6291464 | tf_op jit(solution)/shard_map/ppermute | solution.py:30
  269.7 84.8 %collective-permute-start.10 = (f32[2,256,8,128]{3,2,1,0:T(8,128)S(1)}, f32[2,256,8,128]{3,2,1,0:T(8,128)S(1)}, u32[]{:S(2)}, u32[]{:S(2)}) collective-permute-start(f32[2,256,8,128]{3,2,1,0:T(8,128)S(1)} %bitcast.359), channel_id=1, source_target_pairs={{0,8},{2,10},{4,12},{6,14},{8,0},{10,2},{12,4},{14,6},{16,24},{18,... | collective-permute-start | bytes 6291464 | tf_op jit(solution)/shard_map/ppermute | solution.py:30
  269.8 94.8 %collective-permute-start.11 = (f32[2,256,8,128]{3,2,1,0:T(8,128)S(1)}, f32[2,256,8,128]{3,2,1,0:T(8,128)S(1)}, u32[]{:S(2)}, u32[]{:S(2)}) collective-permute-start(f32[2,256,8,128]{3,2,1,0:T(8,128)S(1)} %bitcast.358), channel_id=1, source_target_pairs={{0,16},{2,18},{4,20},{6,22},{8,24},{10,26},{12,28},{14,30},{16,0},... | collective-permute-start | bytes 6291464 | tf_op jit(solution)/shard_map/ppermute | solution.py:30
  274.5 90.1 %collective-permute-start.8 = (f32[2,256,8,128]{3,2,1,0:T(8,128)S(1)}, f32[2,256,8,128]{3,2,1,0:T(8,128)S(1)}, u32[]{:S(2)}, u32[]{:S(2)}) collective-permute-start(f32[2,256,8,128]{3,2,1,0:T(8,128)S(1)} %bitcast.357), channel_id=1, source_target_pairs={{0,2},{2,0},{4,6},{6,4},{8,10},{10,8},{12,14},{14,12},{16,18},{18,... | collective-permute-start | bytes 6291464 | tf_op jit(solution)/shard_map/ppermute | solution.py:30
  278.7 3.8 collective-permute-start.6
  282.6 43.9 %collective-permute-start.7 = (bf16[2,128,8,128]{3,2,1,0:T(8,128)(2,1)S(1)}, bf16[2,128,8,128]{3,2,1,0:T(8,128)(2,1)S(1)}, u32[]{:S(2)}, u32[]{:S(2)}) collective-permute-start(bf16[2,128,8,128]{3,2,1,0:T(8,128)(2,1)S(1)} %slice.334), channel_id=1, source_target_pairs={{0,2},{2,4},{4,6},{6,8},{8,10},{10,12},{12,14},{14,16},{16,18},{18... | collective-permute-start | bytes 1572872 | tf_op jit(solution)/shard_map/ppermute | solution.py:13
  (4 other events, 3.4 us)
Sparse Core Ops, SparseCore 0:
  10.1 23.9 all-gather.1
  366.9 44.4 reduce-scatter.1
where the time goes:
time: 423 us; the launch traced here: 421 us
  waiting for transfers between devices  129 us (30%)
  local copies, waits for them, and re-layouts  86.9 us (21%)
  starting transfers between devices  82.8 us (20%)
  matrix products  67.9 us (16%)
  other arithmetic  40.2 us (10%)
  between operations  14.5 us (3%)
    ppermute x8, waiting for transfers between devices, swapped(): lax.ppermute(value, axis, [(i, i ^ 1 << distance) for i in range(lax.axis...  58.4 us
    reduce_scatter x1, waiting for transfers between devices, shards(): total = lax.psum_scatter(total, 'head', scatter_dimension=2, tiled=True)  44.7 us
    ppermute x2, starting transfers between devices, from_behind(): lax.ppermute(value, axis, [(source, source + steps) for source in range(i...  43.7 us
    while x4, local copies, waits for them, and re-layouts, shards(): lax.map(one_block, (query_blocks, grad_blocks, key_pairs, valid_all))  39.6 us
    ppermute x8, starting transfers between devices, swapped(): lax.ppermute(value, axis, [(i, i ^ 1 << distance) for i in range(lax.axis...  34.8 us
    dot_general x4, matrix products, shards(): jnp.einsum('jt,jcbhd->ctbhd', routing, level_part, precision=lax.Precisio...  22.6 us
    all_gather x1, waiting for transfers between devices, shards(): all_heads = lax.all_gather(stacked, 'head', axis=2, tiled=True)  22.4 us
    dot_general x4, matrix products, attend(): jnp.einsum('hgqk,qhgd->khd', weights, grad_block, preferred_element_type=...  11.7 us
  transfers between devices with their start and end apart: 14, of which 8 were waited for; matrix products, arithmetic and copies ran while one was open for 6% of the time, Pallas kernels for 0%

commit v1 on v0

v1 whole, which is shorter than its diff:
```python
import functools
import math

import jax
import jax.numpy as jnp
from jax import lax
from jax.experimental import pallas as pl
from jax.experimental.pallas import tpu as pltpu
from jax.sharding import PartitionSpec as P

BLOCK = 128
MESH = pl.DeviceIdType.MESH
NEG = -1e30


def dot(a, b, ca, cb):
    return lax.dot_general(a, b, (((ca,), (cb,)), ((), ())), preferred_element_type=jnp.float32)


def kernel(
    n_seq,
    levels,
    heads,
    table_ref,
    bits_ref,
    query_ref,
    grad_ref,
    kv_ref,
    width_ref,
    out_ref,
    gq_ref,
    dkv_ref,
    query_in,
    grad_in,
    width_in,
    kv_lev,
    kv_rim,
    kv_cat,
    terms,
    out_send,
    gq_send,
    lev_send,
    lev_recv,
    rim_send,
    rim_recv,
    own_sum,
    width_sem,
    qg_sem,
    kv_sem,
    rim_sem,
    og_sem,
    dlev_sem,
    drim_sem,
):
    dev = lax.axis_index("seq")
    head = lax.axis_index("head")
    other = 1 - head
    mine0 = head * heads
    other0 = other * heads
    span = 3
    slots = span + levels
    scale = 128.0 ** (-0.5)
    exp_scale = scale * math.log2(math.e)
    has_low = dev > 0
    has_high = dev < n_seq - 1

    def flip(level):
        step = 1 << level
        return dev + step - 2 * step * (lax.div(dev, step) % 2)

    def remote(src, dst, sems, index, target):
        return pltpu.make_async_remote_copy(
            src_ref=src,
            dst_ref=dst,
            send_sem=sems.at[(0,) + index],
            recv_sem=sems.at[(1,) + index],
            device_id=target,
            device_id_type=MESH,
        )

    barrier = pltpu.get_barrier_semaphore()
    pl.semaphore_signal(barrier, inc=1, device_id=(dev, other), device_id_type=MESH)
    for level in range(levels):
        pl.semaphore_signal(barrier, inc=1, device_id=(flip(level), head), device_id_type=MESH)

    @pl.when(has_low)
    def _():
        pl.semaphore_signal(barrier, inc=1, device_id=(dev - 1, head), device_id_type=MESH)

    @pl.when(has_high)
    def _():
        pl.semaphore_signal(barrier, inc=1, device_id=(dev + 1, head), device_id_type=MESH)

    edges = jnp.where(has_low, 1, 0) + jnp.where(has_high, 1, 0)
    pl.semaphore_wait(barrier, levels + 1 + edges)

    def width_copy():
        return remote(width_ref.at[pl.ds(other0, heads)], width_in, width_sem, (), (dev, other))

    def qg_copies(j):
        return [
            remote(query_ref.at[other0 + j], query_in.at[j], qg_sem, (0, j), (dev, other)),
            remote(grad_ref.at[other0 + j], grad_in.at[j], qg_sem, (1, j), (dev, other)),
        ]

    def kv_copy(j, level):
        return remote(
            kv_ref.at[j], kv_lev.at[level, j], kv_sem, (level, j), (flip(level), head)
        )

    def rim_up(j):
        return remote(
            kv_ref.at[j, :, pl.ds(BLOCK, BLOCK)], kv_rim.at[0, j], rim_sem, (0, j), (dev + 1, head)
        )

    def rim_down(j):
        return remote(
            kv_ref.at[j, :, pl.ds(0, BLOCK)], kv_rim.at[1, j], rim_sem, (1, j), (dev - 1, head)
        )

    def og_copies(j):
        return [
            remote(out_send.at[j], out_ref.at[mine0 + j], og_sem, (0, j), (dev, other)),
            remote(gq_send.at[j], gq_ref.at[mine0 + j], og_sem, (1, j), (dev, other)),
        ]

    def dlev_copy(j, level):
        return remote(
            lev_send.at[level, j], lev_recv.at[level, j], dlev_sem, (level, j), (flip(level), head)
        )

    def drim_up(j):
        return remote(rim_send.at[0, j], rim_recv.at[0, j], drim_sem, (0, j), (dev + 1, head))

    def drim_down(j):
        return remote(rim_send.at[1, j], rim_recv.at[1, j], drim_sem, (1, j), (dev - 1, head))

    width_copy().start()

    def send_head(j, carry):
        for level in reversed(range(levels)):
            kv_copy(j, level).start()

        @pl.when(has_high)
        def _():
            rim_up(j).start()

        @pl.when(has_low)
        def _():
            rim_down(j).start()

        for copy in qg_copies(j):
            copy.start()
        return carry

    lax.fori_loop(0, heads, send_head, 0)

    @pl.when(jnp.logical_not(has_low))
    def _():
        kv_rim[0] = jnp.zeros_like(kv_rim[0])
        rim_recv[0] = jnp.zeros_like(rim_recv[0])

    @pl.when(jnp.logical_not(has_high))
    def _():
        kv_rim[1] = jnp.zeros_like(kv_rim[1])
        rim_recv[1] = jnp.zeros_like(rim_recv[1])

    width_copy().wait_recv()

    chosen = [
        [
            sum(
                (
                    jnp.where(bits_ref[s] == level, table_ref[block, s], 0)
                    for s in range(levels)
                ),
                jnp.int32(0),
            )
            for level in range(levels)
        ]
        for block in range(2)
    ]

    def one_head(j, carry):
        for copy in qg_copies(j):
            copy.wait_recv()
        for level in range(levels):
            kv_copy(j, level).wait_recv()

        @pl.when(has_low)
        def _():
            rim_up(j).wait_recv()

        @pl.when(has_high)
        def _():
            rim_down(j).wait_recv()

        for block in range(2):
            low_ok = has_low if block == 0 else True
            high_ok = has_high if block == 1 else True
            rows = pl.ds(block * 2 * BLOCK, 2 * BLOCK)
            for part in range(2):
                own = kv_ref[j, part]
                band = (
                    [kv_rim[0, j, part], own[:BLOCK], own[BLOCK:]]
                    if block == 0
                    else [own[:BLOCK], own[BLOCK:], kv_rim[1, j, part]]
                )
                for slot in range(span):
                    kv_cat[part, slot * BLOCK : (slot + 1) * BLOCK] = band[slot]
                for level in range(levels):
                    got = kv_lev[level, j, part]
                    pick = jnp.where(chosen[block][level] == 0, got[:BLOCK], got[BLOCK:])
                    kv_cat[part, (span + level) * BLOCK : (span + level + 1) * BLOCK] = pick
            keys = kv_cat[0]
            values = kv_cat[1]
            dk = None
            dv = None
            for source in range(2):
                if source == 0:
                    q = query_ref[mine0 + j, rows]
                    g = grad_ref[mine0 + j, rows]
                    width = width_ref[mine0 + j]
                else:
                    q = query_in[j, rows]
                    g = grad_in[j, rows]
                    width = width_in[j]
                wide = width > 1.5
                low_bias = jnp.where(wide, 0.0, NEG)
                high_bias = low_bias
                if block == 0:
                    low_bias = low_bias + jnp.where(low_ok, 0.0, NEG)
                else:
                    high_bias = high_bias + jnp.where(high_ok, 0.0, NEG)
                reps = 2 * BLOCK // 8
                low_bias = jnp.concatenate([low_bias] * reps, axis=0)
                high_bias = jnp.concatenate([high_bias] * reps, axis=0)
                scores = dot(q, keys, 1, 1)
                scores = jnp.concatenate(
                    [
                        scores[:, :BLOCK] + low_bias,
                        scores[:, BLOCK : 2 * BLOCK],
                        scores[:, 2 * BLOCK : 3 * BLOCK] + high_bias,
                        scores[:, 3 * BLOCK :],
                    ],
                    axis=1,
                )
                top = jnp.max(scores, axis=1, keepdims=True)
                prob = jnp.exp2((scores - top) * exp_scale)
                prob = prob * (1.0 / jnp.sum(prob, axis=1, keepdims=True))
                weights = prob.astype(jnp.bfloat16)
                out = dot(weights, values, 1, 0).astype(jnp.bfloat16)
                delta = jnp.sum(
                    g.astype(jnp.float32) * out.astype(jnp.float32), axis=1, keepdims=True
                )
                ds = (prob * (dot(g, values, 1, 1) - delta)).astype(jnp.bfloat16)
                gq = (dot(ds, keys, 1, 0) * scale).astype(jnp.bfloat16)
                if source == 0:
                    out_ref[mine0 + j, rows] = out
                    gq_ref[mine0 + j, rows] = gq
                else:
                    out_send[j, rows] = out
                    gq_send[j, rows] = gq
                dk_part = dot(ds, q, 0, 0)
                dv_part = dot(weights, g, 0, 0)
                dk = dk_part if dk is None else dk + dk_part
                dv = dv_part if dv is None else dv + dv_part
            terms[block, 0] = dk * scale
            terms[block, 1] = dv

        for copy in og_copies(j):
            copy.start()
        for level in reversed(range(levels)):
            cols = pl.ds((span + level) * BLOCK, BLOCK)
            for part in range(2):
                a = terms[0, part, cols]
                b = terms[1, part, cols]
                for target in range(2):
                    piece = jnp.where(chosen[0][level] == target, a, 0.0) + jnp.where(
                        chosen[1][level] == target, b, 0.0
                    )
                    lev_send[level, j, part, target * BLOCK : (target + 1) * BLOCK] = piece.astype(
                        jnp.bfloat16
                    )
            dlev_copy(j, level).start()
        for part in range(2):
            rim_send[1, j, part] = terms[0, part, :BLOCK].astype(jnp.bfloat16)
            rim_send[0, j, part] = terms[1, part, 2 * BLOCK : 3 * BLOCK].astype(jnp.bfloat16)
            own_sum[j, part, :BLOCK] = terms[0, part, BLOCK : 2 * BLOCK] + terms[1, part, :BLOCK]
            own_sum[j, part, BLOCK:] = (
                terms[0, part, 2 * BLOCK : 3 * BLOCK] + terms[1, part, BLOCK : 2 * BLOCK]
            )

        @pl.when(has_high)
        def _():
            drim_up(j).start()

        @pl.when(has_low)
        def _():
            drim_down(j).start()

        return carry

    lax.fori_loop(0, heads, one_head, 0)

    def finish(j, carry):
        for level in range(levels):
            dlev_copy(j, level).wait_recv()

        @pl.when(has_low)
        def _():
            drim_up(j).wait_recv()

        @pl.when(has_high)
        def _():
            drim_down(j).wait_recv()

        for part in range(2):
            total = own_sum[j, part]
            for level in range(levels):
                total = total + lev_recv[level, j, part].astype(jnp.float32)
            first = total[:BLOCK] + rim_recv[0, j, part].astype(jnp.float32)
            last = total[BLOCK:] + rim_recv[1, j, part].astype(jnp.float32)
            dkv_ref[part, j, :BLOCK] = first.astype(jnp.bfloat16)
            dkv_ref[part, j, BLOCK:] = last.astype(jnp.bfloat16)
        for copy in og_copies(j):
            copy.wait_recv()
        return carry

    lax.fori_loop(0, heads, finish, 0)

    def drain(j, carry):
        for copy in qg_copies(j) + og_copies(j):
            copy.wait_send()
        for level in range(levels):
            kv_copy(j, level).wait_send()
            dlev_copy(j, level).wait_send()

        @pl.when(has_high)
        def _():
            rim_up(j).wait_send()
            drim_up(j).wait_send()

        @pl.when(has_low)
        def _():
            rim_down(j).wait_send()
            drim_down(j).wait_send()

        return carry

    lax.fori_loop(0, heads, drain, 0)
    width_copy().wait_send()


def shards(query, key_in, value, grad_out, band_width, stride_bits, partner_table):
    tokens, kv_heads, groups, dim = query.shape
    heads = key_in.shape[1]
    n_seq = lax.axis_size("seq")
    levels = n_seq.bit_length() - 1
    rows = tokens * groups
    bf16 = jnp.bfloat16
    f32 = jnp.float32
    q = jnp.transpose(query, (1, 0, 2, 3)).reshape(kv_heads, rows, dim)
    g = jnp.transpose(grad_out, (1, 0, 2, 3)).reshape(kv_heads, rows, dim)
    kv = jnp.transpose(jnp.stack([key_in, value]), (2, 0, 1, 3))
    width = jnp.tile(band_width.astype(f32), (1, 8 // groups))
    width = jnp.broadcast_to(width[:, :, None], (kv_heads, 8, 128))
    vmem = pl.BlockSpec(memory_space=pltpu.VMEM)
    smem = pl.BlockSpec(memory_space=pltpu.SMEM)
    slots = 3 + levels
    dma = pltpu.SemaphoreType.DMA
    out, gq, dkv = pl.pallas_call(
        functools.partial(kernel, n_seq, levels, heads),
        out_shape=(
            jax.ShapeDtypeStruct((kv_heads, rows, dim), bf16),
            jax.ShapeDtypeStruct((kv_heads, rows, dim), bf16),
            jax.ShapeDtypeStruct((2, heads, tokens, dim), bf16),
        ),
        in_specs=[smem, smem, vmem, vmem, vmem, vmem],
        out_specs=(vmem, vmem, vmem),
        scratch_shapes=[
            pltpu.VMEM((heads, rows, dim), bf16),
            pltpu.VMEM((heads, rows, dim), bf16),
            pltpu.VMEM((heads, 8, 128), f32),
            pltpu.VMEM((levels, heads, 2, tokens, dim), bf16),
            pltpu.VMEM((2, heads, 2, BLOCK, dim), bf16),
            pltpu.VMEM((2, slots * BLOCK, dim), bf16),
            pltpu.VMEM((2, 2, slots * BLOCK, dim), f32),
            pltpu.VMEM((heads, rows, dim), bf16),
            pltpu.VMEM((heads, rows, dim), bf16),
            pltpu.VMEM((levels, heads, 2, tokens, dim), bf16),
            pltpu.VMEM((levels, heads, 2, tokens, dim), bf16),
            pltpu.VMEM((2, heads, 2, BLOCK, dim), bf16),
            pltpu.VMEM((2, heads, 2, BLOCK, dim), bf16),
            pltpu.VMEM((heads, 2, tokens, dim), f32),
            dma((2,)),
            dma((2, 2, heads)),
            dma((2, levels, heads)),
            dma((2, 2, heads)),
            dma((2, 2, heads)),
            dma((2, levels, heads)),
            dma((2, 2, heads)),
        ],
        compiler_params=pltpu.CompilerParams(
            collective_id=0, has_side_effects=True, vmem_limit_bytes=56 * 1024 * 1024
        ),
    )(partner_table, stride_bits, q, g, kv, width)
    out = jnp.transpose(out.reshape(kv_heads, tokens, groups, dim), (1, 0, 2, 3))
    gq = jnp.transpose(gq.reshape(kv_heads, tokens, groups, dim), (1, 0, 2, 3))
    dkv = jnp.transpose(dkv, (0, 2, 1, 3))
    return out, gq, dkv[0], dkv[1]


def solution(mesh):
    placed = (
        P("seq", None, "head", None),
        P("seq", "head", None),
        P("seq", "head", None),
        P("seq", None, "head", None),
        P(None, "head"),
        P(),
        P("seq", None),
    )
    return jax.shard_map(
        shards,
        mesh=mesh,
        in_specs=placed,
        out_specs=(
            P("seq", None, "head", None),
            P("seq", None, "head", None),
            P("seq", "head", None),
            P("seq", "head", None),
        ),
        check_vma=False,
    )
```

time: 423 us -> 75.7 us (0.18)
  waiting for transfers between devices: 129 us -> 0 us
  starting transfers between devices: 82.8 us -> 0 us
  local copies, waits for them, and re-layouts: 86.9 us -> 12.7 us
  matrix products: 67.9 us -> 0 us
  Pallas kernels: 0 us -> 61.2 us
  other arithmetic: 40.2 us -> 0.85 us
  between operations: 14.5 us -> 0.67 us
    ppermute x12 -> x0, starting transfers between devices: 82.8 us -> none  [the longest x2 43.7 us: from_behind(): lax.ppermute(value, axis, [(source, source + steps) for source in range(i...]
    dot_general x28 -> x0, matrix products: 67.9 us -> none  [the longest x4 22.6 us: shards(): jnp.einsum('jt,jcbhd->ctbhd', routing, level_part, precision=lax.Precisio...]
    ppermute x12 -> x0, waiting for transfers between devices: 61.5 us -> none  [the longest x8 58.4 us: swapped(): lax.ppermute(value, axis, [(i, i ^ 1 << distance) for i in range(lax.axis...]
    pallas_call x0 -> x1, Pallas kernels: none -> 61.2 us  [shards(): pl.pallas_call(functools.partial(kernel, n_seq, levels, heads), out_shape...]
    reduce_scatter x1 -> x0, waiting for transfers between devices: 44.7 us -> none  [shards(): total = lax.psum_scatter(total, 'head', scatter_dimension=2, tiled=True)]
    while x16 -> x0, local copies, waits for them, and re-layouts: 39.7 us -> none  [the longest x4 39.6 us: shards(): lax.map(one_block, (query_blocks, grad_blocks, key_pairs, valid_all))]
    all_gather x1 -> x0, waiting for transfers between devices: 22.4 us -> none  [shards(): all_heads = lax.all_gather(stacked, 'head', axis=2, tiled=True)]
    another operation x14 -> x0, other arithmetic: 14.1 us -> none  [the longest x5 9.68 us: shards(): partner_keys = jnp.stack(partner_list, axis=2)]
  transfers between devices with their start and end apart: 14 -> 0, of which waited for: 8 -> 0; matrix products, arithmetic and copies ran while one was open for 6% -> 0% of each run, Pallas kernels for 0% -> 0%
where the time goes in v1:
time: 75.7 us; the launch traced here: 75.5 us
  Pallas kernels  61.2 us (81%)
  local copies, waits for them, and re-layouts  12.7 us (17%)
  other arithmetic  0.85 us (1%)
    pallas_call x1, Pallas kernels, shards(): pl.pallas_call(functools.partial(kernel, n_seq, levels, heads), out_shape...  61.2 us
    reshape x1, local copies, waits for them, and re-layouts, shards(): out.reshape(kv_heads, tokens, groups, dim)  3 us
    unnamed x12, local copies, waits for them, and re-layouts  2.5 us
    transpose x1, local copies, waits for them, and re-layouts, shards(): q = jnp.transpose(query, (1, 0, 2, 3)).reshape(kv_heads, rows, dim)  1.78 us
    transpose x1, local copies, waits for them, and re-layouts, shards(): g = jnp.transpose(grad_out, (1, 0, 2, 3)).reshape(kv_heads, rows, dim)  1.78 us
    reshape x1, local copies, waits for them, and re-layouts, shards(): gq = jnp.transpose(gq.reshape(kv_heads, tokens, groups, dim), (1, 0, 2, 3))  1.69 us

profile of v1, /device:TPU:0, one launch (start us, length us, event | category | flops | bytes accessed | tf_op | source)
XLA Modules:
  0.0 75.5 jit_solution(2860910534454264763)
XLA Ops:
  0.6 0.0 copy-start.4
  0.6 0.7 copy-done.4
  1.3 0.1 copy.15
  1.4 0.7 broadcast_in_dim.2.width_ref
  2.1 0.0 copy-start
  2.1 1.2 %copy_bitcast_fusion.2 = (bf16[1,256,4,128]{3,1,0,2:T(8,128)(2,1)S(1)}, bf16[1,256,4,128]{3,1,0,2:T(8,128)(2,1)S(1)}) fusion(bf16[256,4,128]{2,1,0:T(4,128)(2,1)} %param.9, bf16[256,4,128]{2,1,0:T(4,128)(2,1)} %param.8), kind=kLoop, calls=%fused_computation.5 | loop fusion | bytes 1048576 | tf_op jit(solution)/shard_map/stack | solution.py:365
  3.3 0.8 %maximum_bitcast_fusion.kv_ref = bf16[4,2,256,128]{3,2,1,0:T(8,128)(2,1)} fusion(bf16[1,256,4,128]{3,1,0,2:T(8,128)(2,1)S(1)} %get-tuple-element.16, bf16[1,256,4,128]{3,1,0,2:T(8,128)(2,1)S(1)} %get-tuple-element.17), kind=kLoop, calls=%fused_computation.2 | loop fusion | flops 262144 | bytes 1048576 | tf_op jit(solution)/shard_map/transpose | solution.py:365
  4.1 0.0 copy-done
  4.1 0.0 copy-start.1
  4.1 1.8 %copy.11 = bf16[8,256,2,128]{3,2,1,0:T(2,128)(2,1)} copy(bf16[8,256,2,128]{3,2,0,1:T(2,128)(2,1)S(1)} %bitcast.26) | data formatting | bytes 2097152 | tf_op jit(solution)/shard_map/transpose | solution.py:363
  5.9 0.0 copy-done.1
  5.9 1.8 %copy.12 = bf16[8,256,2,128]{3,2,1,0:T(2,128)(2,1)} copy(bf16[8,256,2,128]{3,2,0,1:T(2,128)(2,1)S(1)} %bitcast.27) | data formatting | bytes 2097152 | tf_op jit(solution)/shard_map/transpose | solution.py:364
  7.7 61.2 %shard_map.102 = (bf16[8,512,128]{2,1,0:T(8,128)(2,1)}, bf16[8,512,128]{2,1,0:T(8,128)(2,1)}, bf16[2,4,256,128]{3,2,1,0:T(8,128)(2,1)}) custom-call(s32[2,4]{1,0:T(2,128)} %table_ref.1, s32[4]{0:T(128)} %bits_ref.1, bf16[8,512,128]{2,1,0:T(8,128)(2,1)} %bitcast.24, bf16[8,512,128]{2,1,0:T(8,128)(2,1)} %bitcast.25, ...), custom_call_target="tpu_custom_call" | custom-call | tf_op jit(solution)/shard_map/pallas_call | solution.py:372
  68.9 0.0 copy-start.2
  68.9 3.0 %copy.25 = bf16[8,256,2,128]{3,2,0,1:T(2,128)(2,1)} copy(bf16[8,256,2,128]{3,2,1,0:T(2,128)(2,1)} %bitcast.31) | data formatting | bytes 2097152 | tf_op jit(solution)/shard_map/reshape | solution.py:408
  72.0 0.0 copy-done.2
  72.0 0.0 copy-start.3
  72.0 1.7 %copy.24 = bf16[8,256,2,128]{3,2,0,1:T(2,128)(2,1)} copy(bf16[8,256,2,128]{3,2,1,0:T(2,128)(2,1)S(1)} %bitcast.30) | data formatting | bytes 2097152 | tf_op jit(solution)/shard_map/reshape | solution.py:409
  73.6 0.0 copy-done.3
  73.7 0.9 %copy.19 = bf16[256,4,128]{2,1,0:T(4,128)(2,1)} copy(bf16[256,4,128]{2,0,1:T(8,128)(2,1)S(1)} %get-tuple-element.14) | data formatting | bytes 524288
  74.6 0.9 %copy.18 = bf16[256,4,128]{2,1,0:T(4,128)(2,1)} copy(bf16[256,4,128]{2,0,1:T(8,128)(2,1)S(1)} %get-tuple-element.15) | data formatting | bytes 524288
  (3 shorter events, 0.0 us)
Async XLA Ops:
  0.6 0.7 copy-start.4
  2.1 2.0 %copy-start = (bf16[256,8,2,128]{3,2,1,0:T(2,128)(2,1)S(1)}, bf16[256,8,2,128]{3,2,1,0:T(2,128)(2,1)}, u32[]{:S(2)}) copy-start(bf16[256,8,2,128]{3,2,1,0:T(2,128)(2,1)} %param.7) | copy-start | bytes 3145732
  4.1 1.8 %copy-start.1 = (bf16[256,8,2,128]{3,2,1,0:T(2,128)(2,1)S(1)}, bf16[256,8,2,128]{3,2,1,0:T(2,128)(2,1)}, u32[]{:S(2)}) copy-start(bf16[256,8,2,128]{3,2,1,0:T(2,128)(2,1)} %param.10) | copy-start | bytes 3145732
  68.9 3.0 %copy-start.2 = (bf16[8,512,128]{2,1,0:T(8,128)(2,1)S(1)}, bf16[8,512,128]{2,1,0:T(8,128)(2,1)}, u32[]{:S(2)}) copy-start(bf16[8,512,128]{2,1,0:T(8,128)(2,1)} %get-tuple-element.8) | copy-start | bytes 3145732
  72.0 1.7 %copy-start.3 = (bf16[2,4,256,128]{3,2,1,0:T(8,128)(2,1)S(1)}, bf16[2,4,256,128]{3,2,1,0:T(8,128)(2,1)}, u32[]{:S(2)}) copy-start(bf16[2,4,256,128]{3,2,1,0:T(8,128)(2,1)} %get-tuple-element.9) | copy-start | bytes 1572868

commit v2 on v1

--- a/solution.py
+++ b/solution.py
@@ -21,15 +21,19 @@
     n_seq,
     levels,
     heads,
+    groups,
     table_ref,
     bits_ref,
     query_ref,
     grad_ref,
-    kv_ref,
+    key_ref,
+    value_ref,
     width_ref,
     out_ref,
     gq_ref,
-    dkv_ref,
+    dk_ref,
+    dv_ref,
+    kv_ref,
     query_in,
     grad_in,
     width_in,
@@ -95,7 +99,7 @@
     pl.semaphore_wait(barrier, levels + 1 + edges)
 
     def width_copy():
-        return remote(width_ref.at[pl.ds(other0, heads)], width_in, width_sem, (), (dev, other))
+        return remote(width_ref, width_in, width_sem, (), (dev, other))
 
     def qg_copies(j):
         return [
@@ -118,10 +122,15 @@
             kv_ref.at[j, :, pl.ds(0, BLOCK)], kv_rim.at[1, j], rim_sem, (1, j), (dev - 1, head)
         )
 
-    def og_copies(j):
+    def og_copies(j, block):
+        rows = pl.ds(block * 2 * BLOCK, 2 * BLOCK)
         return [
-            remote(out_send.at[j], out_ref.at[mine0 + j], og_sem, (0, j), (dev, other)),
-            remote(gq_send.at[j], gq_ref.at[mine0 + j], og_sem, (1, j), (dev, other)),
+            remote(
+                out_send.at[j, rows], out_ref.at[mine0 + j, rows], og_sem, (0, block, j), (dev, other)
+            ),
+            remote(
+                gq_send.at[j, rows], gq_ref.at[mine0 + j, rows], og_sem, (1, block, j), (dev, other)
+            ),
         ]
 
     def dlev_copy(j, level):
@@ -135,25 +144,25 @@
     def drim_down(j):
         return remote(rim_send.at[1, j], rim_recv.at[1, j], drim_sem, (1, j), (dev - 1, head))
 
-    width_copy().start()
-
-    def send_head(j, carry):
+    def send_head(j):
+        kv_ref[j, 0] = key_ref[j]
+        kv_ref[j, 1] = value_ref[j]
+
+        @pl.when(has_high)
+        def _():
+            rim_up(j).start()
+
+        @pl.when(has_low)
+        def _():
+            rim_down(j).start()
+
         for level in reversed(range(levels)):
             kv_copy(j, level).start()
-
-        @pl.when(has_high)
-        def _():
-            rim_up(j).start()
-
-        @pl.when(has_low)
-        def _():
-            rim_down(j).start()
-
         for copy in qg_copies(j):
             copy.start()
-        return carry
-
-    lax.fori_loop(0, heads, send_head, 0)
+
+    send_head(0)
+    width_copy().start()
 
     @pl.when(jnp.logical_not(has_low))
     def _():
@@ -182,10 +191,17 @@
     ]
 
     def one_head(j, carry):
+        for level in range(min(2, levels)):
+            kv_copy(j, level).wait_recv()
+
+        @pl.when(j == 0)
+        def _():
+            send_head(1)
+
+        for level in range(min(2, levels), levels):
+            kv_copy(j, level).wait_recv()
         for copy in qg_copies(j):
             copy.wait_recv()
-        for level in range(levels):
-            kv_copy(j, level).wait_recv()
 
         @pl.when(has_low)
         def _():
@@ -194,6 +210,10 @@
         @pl.when(has_high)
         def _():
             rim_down(j).wait_recv()
+
+        @pl.when(j + 2 < heads)
+        def _():
+            send_head(j + 2)
 
         for block in range(2):
             low_ok = has_low if block == 0 else True
@@ -220,12 +240,16 @@
                 if source == 0:
                     q = query_ref[mine0 + j, rows]
                     g = grad_ref[mine0 + j, rows]
-                    width = width_ref[mine0 + j]
+                    width = width_ref[pl.ds(mine0 + j, 1)]
                 else:
                     q = query_in[j, rows]
                     g = grad_in[j, rows]
-                    width = width_in[j]
-                wide = width > 1.5
+                    width = width_in[pl.ds(mine0 + j, 1)]
+                lane = lax.broadcasted_iota(jnp.int32, (8, 128), 0) % groups
+                wide = jnp.zeros((8, 128), jnp.int32)
+                for group in range(groups):
+                    wide = jnp.where(lane == group, width[:, group : group + 1], wide)
+                wide = wide > 1
                 low_bias = jnp.where(wide, 0.0, NEG)
                 high_bias = low_bias
                 if block == 0:
@@ -267,9 +291,26 @@
                 dv = dv_part if dv is None else dv + dv_part
             terms[block, 0] = dk * scale
             terms[block, 1] = dv
-
-        for copy in og_copies(j):
-            copy.start()
+            for copy in og_copies(j, block):
+                copy.start()
+            if block == 0:
+                for part in range(2):
+                    rim_send[1, j, part] = terms[0, part, :BLOCK].astype(jnp.bfloat16)
+
+                @pl.when(has_low)
+                def _():
+                    drim_down(j).start()
+
+            else:
+                for part in range(2):
+                    rim_send[0, j, part] = terms[1, part, 2 * BLOCK : 3 * BLOCK].astype(
+                        jnp.bfloat16
+                    )
+
+                @pl.when(has_high)
+                def _():
+                    drim_up(j).start()
+
         for level in reversed(range(levels)):
             cols = pl.ds((span + level) * BLOCK, BLOCK)
             for part in range(2):
@@ -284,20 +325,10 @@
                     )
             dlev_copy(j, level).start()
         for part in range(2):
-            rim_send[1, j, part] = terms[0, part, :BLOCK].astype(jnp.bfloat16)
-            rim_send[0, j, part] = terms[1, part, 2 * BLOCK : 3 * BLOCK].astype(jnp.bfloat16)
             own_sum[j, part, :BLOCK] = terms[0, part, BLOCK : 2 * BLOCK] + terms[1, part, :BLOCK]
             own_sum[j, part, BLOCK:] = (
                 terms[0, part, 2 * BLOCK : 3 * BLOCK] + terms[1, part, BLOCK : 2 * BLOCK]
             )
-
-        @pl.when(has_high)
-        def _():
-            drim_up(j).start()
-
-        @pl.when(has_low)
-        def _():
-            drim_down(j).start()
 
         return carry
 
@@ -321,16 +352,18 @@
                 total = total + lev_recv[level, j, part].astype(jnp.float32)
             first = total[:BLOCK] + rim_recv[0, j, part].astype(jnp.float32)
             last = total[BLOCK:] + rim_recv[1, j, part].astype(jnp.float32)
-            dkv_ref[part, j, :BLOCK] = first.astype(jnp.bfloat16)
-            dkv_ref[part, j, BLOCK:] = last.astype(jnp.bfloat16)
-        for copy in og_copies(j):
-            copy.wait_recv()
+            result = (dk_ref, dv_ref)[part]
+            result[j, :BLOCK] = first.astype(jnp.bfloat16)
+            result[j, BLOCK:] = last.astype(jnp.bfloat16)
+        for block in range(2):
+            for copy in og_copies(j, block):
+                copy.wait_recv()
         return carry
 
     lax.fori_loop(0, heads, finish, 0)
 
     def drain(j, carry):
-        for copy in qg_copies(j) + og_copies(j):
+        for copy in qg_copies(j) + og_copies(j, 0) + og_copies(j, 1):
             copy.wait_send()
         for level in range(levels):
             kv_copy(j, level).wait_send()
@@ -362,26 +395,28 @@
     f32 = jnp.float32
     q = jnp.transpose(query, (1, 0, 2, 3)).reshape(kv_heads, rows, dim)
     g = jnp.transpose(grad_out, (1, 0, 2, 3)).reshape(kv_heads, rows, dim)
-    kv = jnp.transpose(jnp.stack([key_in, value]), (2, 0, 1, 3))
-    width = jnp.tile(band_width.astype(f32), (1, 8 // groups))
-    width = jnp.broadcast_to(width[:, :, None], (kv_heads, 8, 128))
+    k = jnp.transpose(key_in, (1, 0, 2))
+    v = jnp.transpose(value, (1, 0, 2))
+    width = jnp.pad(band_width, ((0, 0), (0, 128 - groups)))
     vmem = pl.BlockSpec(memory_space=pltpu.VMEM)
     smem = pl.BlockSpec(memory_space=pltpu.SMEM)
     slots = 3 + levels
     dma = pltpu.SemaphoreType.DMA
-    out, gq, dkv = pl.pallas_call(
-        functools.partial(kernel, n_seq, levels, heads),
+    out, gq, dk, dv = pl.pallas_call(
+        functools.partial(kernel, n_seq, levels, heads, groups),
         out_shape=(
             jax.ShapeDtypeStruct((kv_heads, rows, dim), bf16),
             jax.ShapeDtypeStruct((kv_heads, rows, dim), bf16),
-            jax.ShapeDtypeStruct((2, heads, tokens, dim), bf16),
+            jax.ShapeDtypeStruct((heads, tokens, dim), bf16),
+            jax.ShapeDtypeStruct((heads, tokens, dim), bf16),
         ),
-        in_specs=[smem, smem, vmem, vmem, vmem, vmem],
-        out_specs=(vmem, vmem, vmem),
+        in_specs=[smem, smem] + [vmem] * 5,
+        out_specs=(vmem,) * 4,
         scratch_shapes=[
+            pltpu.VMEM((heads, 2, tokens, dim), bf16),
             pltpu.VMEM((heads, rows, dim), bf16),
             pltpu.VMEM((heads, rows, dim), bf16),
-            pltpu.VMEM((heads, 8, 128), f32),
+            pltpu.VMEM((kv_heads, 128), jnp.int32),
             pltpu.VMEM((levels, heads, 2, tokens, dim), bf16),
             pltpu.VMEM((2, heads, 2, BLOCK, dim), bf16),
             pltpu.VMEM((2, slots * BLOCK, dim), bf16),
@@ -397,18 +432,17 @@
             dma((2, 2, heads)),
             dma((2, levels, heads)),
             dma((2, 2, heads)),
-            dma((2, 2, heads)),
+            dma((2, 2, 2, heads)),
             dma((2, levels, heads)),
             dma((2, 2, heads)),
         ],
         compiler_params=pltpu.CompilerParams(
-            collective_id=0, has_side_effects=True, vmem_limit_bytes=56 * 1024 * 1024
+            collective_id=0, has_side_effects=True, vmem_limit_bytes=34 * 1024 * 1024
         ),
-    )(partner_table, stride_bits, q, g, kv, width)
+    )(partner_table, stride_bits, q, g, k, v, width)
     out = jnp.transpose(out.reshape(kv_heads, tokens, groups, dim), (1, 0, 2, 3))
     gq = jnp.transpose(gq.reshape(kv_heads, tokens, groups, dim), (1, 0, 2, 3))
-    dkv = jnp.transpose(dkv, (0, 2, 1, 3))
-    return out, gq, dkv[0], dkv[1]
+    return out, gq, jnp.transpose(dk, (1, 0, 2)), jnp.transpose(dv, (1, 0, 2))
 
 
 def solution(mesh):

time: 75.7 us -> 71.5 us (0.945)
  local copies, waits for them, and re-layouts: 12.7 us -> 9.75 us
  other arithmetic: 0.85 us -> 0 us
    unnamed x12 -> x11, local copies, waits for them, and re-layouts: 2.5 us -> 3.82 us
    reshape x1, local copies, waits for them, and re-layouts: 3 us -> 1.69 us  [shards(): out.reshape(kv_heads, tokens, groups, dim)]
    another operation x3 -> x0, local copies, waits for them, and re-layouts: 1.27 us -> none  [the longest x1 1.19 us: shards(): kv = jnp.transpose(jnp.stack([key_in, value]), (2, 0, 1, 3))]
    transpose x0 -> x1, local copies, waits for them, and re-layouts: none -> 1.1 us  [shards(): v = jnp.transpose(value, (1, 0, 2))]
    transpose x1, local copies, waits for them, and re-layouts: 1.78 us -> 0.72 us  [shards(): g = jnp.transpose(grad_out, (1, 0, 2, 3)).reshape(kv_heads, rows, dim)]
    transpose x1, local copies, waits for them, and re-layouts: 1.78 us -> 0.72 us  [shards(): q = jnp.transpose(query, (1, 0, 2, 3)).reshape(kv_heads, rows, dim)]
    transpose x1 -> x0, other arithmetic: 0.85 us -> none  [shards(): kv = jnp.transpose(jnp.stack([key_in, value]), (2, 0, 1, 3))]
where the time goes in v2:
time: 71.5 us; the launch traced here: 71.3 us
  Pallas kernels  60.8 us (85%)
  local copies, waits for them, and re-layouts  9.75 us (14%)
    pallas_call x1, Pallas kernels, shards(): pl.pallas_call(functools.partial(kernel, n_seq, levels, heads, groups), o...  60.8 us
    unnamed x11, local copies, waits for them, and re-layouts  3.82 us
    reshape x1, local copies, waits for them, and re-layouts, shards(): out.reshape(kv_heads, tokens, groups, dim)  1.69 us
    reshape x1, local copies, waits for them, and re-layouts, shards(): gq = jnp.transpose(gq.reshape(kv_heads, tokens, groups, dim), (1, 0, 2, 3))  1.69 us

profile of v2, /device:TPU:0, one launch (start us, length us, event | category | flops | bytes accessed | tf_op | source)
XLA Modules:
  0.0 71.3 jit_solution(15719816104629290875)
XLA Ops:
  0.6 0.0 copy-start.2
  0.6 0.8 %copy.15 = s32[8,2]{1,0:T(8,128)S(1)} copy(s32[8,2]{0,1:T(2,128)} %param.11) | data formatting | bytes 128 | tf_op args[4]
  1.5 1.1 %copy_bitcast_fusion.2 = (bf16[4,256,128]{2,1,0:T(8,128)(2,1)S(1)}, bf16[4,256,128]{2,1,0:T(8,128)(2,1)S(1)}) fusion(bf16[256,4,128]{2,1,0:T(4,128)(2,1)} %param.9, bf16[256,4,128]{2,1,0:T(4,128)(2,1)} %param.8), kind=kLoop, calls=%fused_computation.2 | loop fusion | bytes 1048576 | tf_op jit(solution)/shard_map/transpose | solution.py:399
  2.6 0.0 copy-done.2
  2.6 0.0 copy-start.3
  2.6 0.7 %copy.11 = bf16[8,256,2,128]{3,2,1,0:T(2,128)(2,1)S(1)} copy(bf16[8,256,2,128]{3,2,0,1:T(2,128)(2,1)S(1)} %bitcast.24) | data formatting | bytes 2097152 | tf_op jit(solution)/shard_map/transpose | solution.py:396
  3.3 0.5 copy-done.3
  3.8 0.7 %copy.12 = bf16[8,256,2,128]{3,2,1,0:T(2,128)(2,1)S(1)} copy(bf16[8,256,2,128]{3,2,0,1:T(2,128)(2,1)S(1)} %bitcast.25) | data formatting | bytes 2097152 | tf_op jit(solution)/shard_map/transpose | solution.py:397
  4.6 0.0 copy-start
  4.6 0.0 copy-start.1
  4.6 0.7 copy-done
  5.2 0.0 copy-done.1
  5.2 60.8 %shard_map.102 = (bf16[8,512,128]{2,1,0:T(8,128)(2,1)S(1)}, bf16[8,512,128]{2,1,0:T(8,128)(2,1)S(1)}, bf16[4,256,128]{2,1,0:T(8,128)(2,1)S(1)}, bf16[4,256,128]{2,1,0:T(8,128)(2,1)S(1)}) custom-call(s32[2,4]{1,0:T(2,128)S(1)} %copy-done, s32[4]{0:T(128)S(1)} %copy-done.1, bf16[8,512,128]{2,1,0:T(8,128)(2,1)S(1)} %bitcast.18, ...), custom_call_target="tpu_custom_call" | custom-call | tf_op jit(solution)/shard_map/pallas_call | solution.py:405
  66.1 1.7 %copy.25 = bf16[8,256,2,128]{3,2,0,1:T(2,128)(2,1)} copy(bf16[8,256,2,128]{3,2,1,0:T(2,128)(2,1)S(1)} %bitcast.21) | data formatting | bytes 2097152 | tf_op jit(solution)/shard_map/reshape | solution.py:443
  67.8 1.7 %copy.24 = bf16[8,256,2,128]{3,2,0,1:T(2,128)(2,1)} copy(bf16[8,256,2,128]{3,2,1,0:T(2,128)(2,1)S(1)} %bitcast.20) | data formatting | bytes 2097152 | tf_op jit(solution)/shard_map/reshape | solution.py:444
  69.4 0.9 %copy.18 = bf16[256,4,128]{2,1,0:T(4,128)(2,1)} copy(bf16[256,4,128]{2,0,1:T(8,128)(2,1)S(1)} %bitcast.23) | data formatting | bytes 524288
  70.4 0.9 %copy.19 = bf16[256,4,128]{2,1,0:T(4,128)(2,1)} copy(bf16[256,4,128]{2,0,1:T(8,128)(2,1)S(1)} %bitcast.22) | data formatting | bytes 524288
  (1 shorter events, 0.0 us)
Async XLA Ops:
  0.6 2.0 %copy-start.2 = (bf16[256,8,2,128]{3,2,1,0:T(2,128)(2,1)S(1)}, bf16[256,8,2,128]{3,2,1,0:T(2,128)(2,1)}, u32[]{:S(2)}) copy-start(bf16[256,8,2,128]{3,2,1,0:T(2,128)(2,1)} %param.7) | copy-start | bytes 3145732
  2.6 1.2 %copy-start.3 = (bf16[256,8,2,128]{3,2,1,0:T(2,128)(2,1)S(1)}, bf16[256,8,2,128]{3,2,1,0:T(2,128)(2,1)}, u32[]{:S(2)}) copy-start(bf16[256,8,2,128]{3,2,1,0:T(2,128)(2,1)} %param.10) | copy-start | bytes 3145732
  4.6 0.7 copy-start
  4.6 0.7 copy-start.1

commit v3 on v2

--- a/solution.py
+++ b/solution.py
@@ -285,12 +285,12 @@
                 else:
                     out_send[j, rows] = out
                     gq_send[j, rows] = gq
-                dk_part = dot(ds, q, 0, 0)
-                dv_part = dot(weights, g, 0, 0)
+                dk_part = dot(q, ds, 0, 0)
+                dv_part = dot(g, weights, 0, 0)
                 dk = dk_part if dk is None else dk + dk_part
                 dv = dv_part if dv is None else dv + dv_part
-            terms[block, 0] = dk * scale
-            terms[block, 1] = dv
+            terms[block, 0] = (dk * scale).T
+            terms[block, 1] = dv.T
             for copy in og_copies(j, block):
                 copy.start()
             if block == 0:

time: 71.5 us -> 71.5 us (level)
  no operation moved by 1% of the time
where the time goes in v3:
time: 71.5 us; the launch traced here: 71.3 us
  Pallas kernels  60.8 us (85%)
  local copies, waits for them, and re-layouts  9.75 us (14%)
    pallas_call x1, Pallas kernels, shards(): pl.pallas_call(functools.partial(kernel, n_seq, levels, heads, groups), o...  60.8 us
    unnamed x11, local copies, waits for them, and re-layouts  3.82 us
    reshape x1, local copies, waits for them, and re-layouts, shards(): out.reshape(kv_heads, tokens, groups, dim)  1.69 us
    reshape x1, local copies, waits for them, and re-layouts, shards(): gq = jnp.transpose(gq.reshape(kv_heads, tokens, groups, dim), (1, 0, 2, 3))  1.69 us

profile of v3, /device:TPU:0, one launch (start us, length us, event | category | flops | bytes accessed | tf_op | source)
XLA Modules:
  0.0 71.3 jit_solution(4517758267930355267)
XLA Ops:
  0.6 0.0 copy-start.2
  0.6 0.8 %copy.15 = s32[8,2]{1,0:T(8,128)S(1)} copy(s32[8,2]{0,1:T(2,128)} %param.11) | data formatting | bytes 128 | tf_op args[4]
  1.5 1.1 %copy_bitcast_fusion.2 = (bf16[4,256,128]{2,1,0:T(8,128)(2,1)S(1)}, bf16[4,256,128]{2,1,0:T(8,128)(2,1)S(1)}) fusion(bf16[256,4,128]{2,1,0:T(4,128)(2,1)} %param.9, bf16[256,4,128]{2,1,0:T(4,128)(2,1)} %param.8), kind=kLoop, calls=%fused_computation.2 | loop fusion | bytes 1048576 | tf_op jit(solution)/shard_map/transpose | solution.py:399
  2.6 0.0 copy-done.2
  2.6 0.0 copy-start.3
  2.6 0.7 %copy.11 = bf16[8,256,2,128]{3,2,1,0:T(2,128)(2,1)S(1)} copy(bf16[8,256,2,128]{3,2,0,1:T(2,128)(2,1)S(1)} %bitcast.24) | data formatting | bytes 2097152 | tf_op jit(solution)/shard_map/transpose | solution.py:396
  3.3 0.5 copy-done.3
  3.8 0.7 %copy.12 = bf16[8,256,2,128]{3,2,1,0:T(2,128)(2,1)S(1)} copy(bf16[8,256,2,128]{3,2,0,1:T(2,128)(2,1)S(1)} %bitcast.25) | data formatting | bytes 2097152 | tf_op jit(solution)/shard_map/transpose | solution.py:397
  4.6 0.0 copy-start
  4.6 0.0 copy-start.1
  4.6 0.7 copy-done
  5.2 0.0 copy-done.1
  5.2 60.8 %shard_map.102 = (bf16[8,512,128]{2,1,0:T(8,128)(2,1)S(1)}, bf16[8,512,128]{2,1,0:T(8,128)(2,1)S(1)}, bf16[4,256,128]{2,1,0:T(8,128)(2,1)S(1)}, bf16[4,256,128]{2,1,0:T(8,128)(2,1)S(1)}) custom-call(s32[2,4]{1,0:T(2,128)S(1)} %copy-done, s32[4]{0:T(128)S(1)} %copy-done.1, bf16[8,512,128]{2,1,0:T(8,128)(2,1)S(1)} %bitcast.18, ...), custom_call_target="tpu_custom_call" | custom-call | tf_op jit(solution)/shard_map/pallas_call | solution.py:405
  66.1 1.7 %copy.25 = bf16[8,256,2,128]{3,2,0,1:T(2,128)(2,1)} copy(bf16[8,256,2,128]{3,2,1,0:T(2,128)(2,1)S(1)} %bitcast.21) | data formatting | bytes 2097152 | tf_op jit(solution)/shard_map/reshape | solution.py:443
  67.8 1.7 %copy.24 = bf16[8,256,2,128]{3,2,0,1:T(2,128)(2,1)} copy(bf16[8,256,2,128]{3,2,1,0:T(2,128)(2,1)S(1)} %bitcast.20) | data formatting | bytes 2097152 | tf_op jit(solution)/shard_map/reshape | solution.py:444
  69.4 0.9 %copy.18 = bf16[256,4,128]{2,1,0:T(4,128)(2,1)} copy(bf16[256,4,128]{2,0,1:T(8,128)(2,1)S(1)} %bitcast.23) | data formatting | bytes 524288
  70.4 0.9 %copy.19 = bf16[256,4,128]{2,1,0:T(4,128)(2,1)} copy(bf16[256,4,128]{2,0,1:T(8,128)(2,1)S(1)} %bitcast.22) | data formatting | bytes 524288
  (1 shorter events, 0.0 us)
Async XLA Ops:
  0.6 2.0 %copy-start.2 = (bf16[256,8,2,128]{3,2,1,0:T(2,128)(2,1)S(1)}, bf16[256,8,2,128]{3,2,1,0:T(2,128)(2,1)}, u32[]{:S(2)}) copy-start(bf16[256,8,2,128]{3,2,1,0:T(2,128)(2,1)} %param.7) | copy-start | bytes 3145732
  2.6 1.2 %copy-start.3 = (bf16[256,8,2,128]{3,2,1,0:T(2,128)(2,1)S(1)}, bf16[256,8,2,128]{3,2,1,0:T(2,128)(2,1)}, u32[]{:S(2)}) copy-start(bf16[256,8,2,128]{3,2,1,0:T(2,128)(2,1)} %param.10) | copy-start | bytes 3145732
  4.6 0.7 copy-start
  4.6 0.7 copy-start.1
